TPU v7x, 512 devices: a whole 4x4x16 slice. The times are simulated.
512 devices in a mesh: feat: 64 (over z_lo, y, core), tok: 8 (over z_hi, x).
Axes of the slice: x: 4, y: 4, z: 16 (z_hi: 2, z_lo: 8; z = z_hi * 8 + z_lo), core: 2. Of those that a mesh axis runs over, the one named last changes fastest.
Arguments:
- source: bfloat16 [1024, 3584], P(('tok', 'feat')), may hold values from -6 to 6
- target: bfloat16 [1024, 3584], P(('tok', 'feat')), may hold values from -6 to 6
- enc_weight: bfloat16 [3584, 16384], P('tok', 'feat'), may hold values from -0.09375 to 0.09375
- enc_bias: float32 [16384], P('feat'), may hold values from -3 to 3
- dec_weight: bfloat16 [16384, 3584], P('feat', 'tok'), may hold values from -0.09375 to 0.09375
- active: int32 [1024, 16384], P('tok', 'feat'), may hold values 0 or 1
Outputs:
- recon_error: float32 [1024, 3584], P(('tok', 'feat'))
- grad_enc: bfloat16 [3584, 16384], P(None, 'feat')
- grad_bias: float32 [16384], P('feat')
- grad_dec: bfloat16 [16384, 3584], P('feat')
All inputs are finite; a program needn't handle non-finite values. No bound on the sum of `active` on one device may be relied on, other than what follows from the above.
Results may differ from a plain program's by a relative error of at most 0.019.
Values may be sent and summed in bfloat16 or wider, within the bound.
A program may use at most 64 MiB of HBM per device.

v0:
```python
import math

import jax
import jax.numpy as jnp
from jax import lax
from jax.sharding import PartitionSpec as P


def on_device(source, target, enc_weight, enc_bias, dec_weight, active):
    row_count = source.shape[0]
    group_rows = row_count * lax.axis_size("feat")
    token_total = group_rows * lax.axis_size("tok")
    gathered = lax.all_gather(source, "feat", axis=0, tiled=True)
    slab_rows = gathered
    preact = (
        jnp.dot(
            slab_rows,
            lax.all_gather(enc_weight, "tok", axis=0, tiled=True),
            preferred_element_type=jnp.float32,
        )
        + enc_bias
    )
    gating = active.astype(jnp.float32)
    features = (gating * preact).astype(jnp.bfloat16)
    full_dec = lax.all_gather(dec_weight, "tok", axis=1, tiled=True)
    slab_rows = features
    recon = lax.psum_scatter(
        jnp.dot(slab_rows, full_dec, preferred_element_type=jnp.float32),
        "feat",
        scatter_dimension=0,
        tiled=True,
    )
    recon_error = recon - target.astype(jnp.float32)
    signal = (recon_error * (1.0 / math.sqrt(token_total))).astype(jnp.bfloat16)
    signal_all = lax.all_gather(signal, "feat", axis=0, tiled=True)
    dec_part = lax.dot_general(
        features, signal_all, (((0,), (0,)), ((), ())), preferred_element_type=jnp.float32
    )
    backflow = lax.dot_general(
        signal_all, full_dec, (((1,), (1,)), ((), ())), preferred_element_type=jnp.float32
    )
    pre_grad = gating * backflow
    pre_round = pre_grad.astype(jnp.bfloat16)
    bias_part = jnp.sum(pre_grad, axis=0).astype(jnp.bfloat16)
    enc_part = lax.dot_general(
        gathered, pre_round, (((0,), (0,)), ((), ())), preferred_element_type=jnp.float32
    )
    enc_half = enc_part.astype(jnp.bfloat16)
    dec_half = dec_part.astype(jnp.bfloat16)
    enc_summed, dec_summed, bias_summed = (
        lax.psum(enc_half, "tok").astype(jnp.float32),
        lax.psum(dec_half, "tok").astype(jnp.float32),
        lax.psum(bias_part, "tok").astype(jnp.float32),
    )
    enc_out = enc_summed.astype(jnp.bfloat16)
    dec_out = dec_summed.astype(jnp.bfloat16)
    return (recon_error, enc_out, bias_summed, dec_out)


def solution(mesh):
    placed = (
        P(("tok", "feat"), None),
        P(("tok", "feat"), None),
        P("tok", "feat"),
        P("feat"),
        P("feat", "tok"),
        P("tok", "feat"),
    )
    return jax.shard_map(
        on_device,
        mesh=mesh,
        in_specs=placed,
        out_specs=(P(("tok", "feat"), None), P(None, "feat"), P("feat"), P("feat", None)),
        check_vma=False,
    )
```

profile of v0, /device:TPU:1, one launch (start us, length us, event | category | flops | bytes accessed | tf_op | source)
XLA Modules:
  0.0 1522.7 jit_solution(12357005956135973958)
XLA Ops:
  7.2 0.0 copy-start.2
  7.2 0.0 copy-start.4
  7.2 0.0 all-gather.5.cloned.1.call-start
  7.2 0.7 all-gather.5.cloned.1.call-update
  7.9 0.0 all-gather.7.cloned.1.call-start
  8.0 0.7 all-gather.7.cloned.1.call-update
  8.7 0.0 all-reduce.5.cloned.1.call-start
  8.7 148.6 %all-gather = bf16[64,2,3584]{2,1,0:T(2,128)(2,1)S(1)} all-gather(bf16[1,2,3584]{2,1,0:T(2,128)(2,1)} %bitcast.16), channel_id=1, replica_groups=mesh['feat'=64,'tok'=8] {'feat'}, dimensions={0}, use_global_device_ids=true | all-gather | bytes 931840 | tf_op jit(solution)/shard_map/all_gather | solution.py:13
  157.3 0.3 reshape.10
  157.6 0.0 all-gather.5.cloned.1.call-done
  157.7 0.0 copy-done.2
  157.7 0.0 copy-done.4
  157.7 1.9 fusion.2
  159.6 74.7 %all-gather.7.cloned.1.call-done = bf16[256,3584]{0,1:T(8,128)(2,1)} async-done(((bf16[256,448]{0,1:T(8,128)(2,1)}), bf16[256,3584]{0,1:T(8,128)(2,1)}) %all-gather.7.cloned.1.call-update) | async-done | bytes 1835024 | tf_op jit(solution)/shard_map/all_gather | solution.py:25
  234.3 3.5 fusion.6
  237.7 0.0 copy-start.3
  237.7 0.0 all-reduce.5.cloned.1.call-update
  237.8 0.0 all-reduce.7.cloned.1.call-start
  237.8 1.3 dynamic-slice
  239.7 811.7 %all-reduce.5.cloned.1.call-done = f32[128,3584]{1,0:T(8,128)} async-done(((f32[128,3584]{1,0:T(8,128)}), f32[128,3584]{1,0:T(8,128)}) %all-reduce.5.cloned.1.call-update) | async-done | bytes 1835024
  1051.4 0.0 copy-done.3
  1051.4 1.5 fusion.4
  1052.9 123.9 %all-gather.1 = bf16[64,2,3584]{2,1,0:T(2,128)(2,1)S(1)} all-gather(bf16[1,2,3584]{2,1,0:T(2,128)(2,1)S(1)} %get-tuple-element.14), channel_id=1, replica_groups=mesh['feat'=64,'tok'=8] {'feat'}, dimensions={0}, use_global_device_ids=true | all-gather | bytes 931840 | tf_op jit(solution)/shard_map/all_gather | solution.py:35
  1176.8 0.3 reshape.12
  1177.2 0.0 copy-start
  1177.2 1.9 convolution_convert_fusion
  1179.1 0.0 copy-done
  1179.1 0.4 fusion.5
  1179.5 1.9 fusion
  1181.4 0.0 all-reduce.7.cloned.1.call-update
  1181.4 38.3 %psum.22 = bf16[256]{0:T(256)(128)(2,1)S(1)} all-reduce(bf16[256]{0:T(256)(128)(2,1)S(1)} %get-tuple-element.16), channel_id=1, replica_groups=mesh['feat'=64,'tok'=8] {'tok'}, use_global_device_ids=true, to_apply=%region_3.0 | all-reduce | flops 256 | bytes 1024 | tf_op jit(solution)/shard_map/psum | solution.py:53
  1219.7 0.6 convert_element_type.42
  1220.3 290.8 %all-reduce.7.cloned.1.call-done = (bf16[3584,256]{0,1:T(8,128)(2,1)}, bf16[256,3584]{1,0:T(8,128)(2,1)}) async-done(((bf16[3584,256]{0,1:T(8,128)(2,1)}, bf16[256,3584]{1,0:T(8,128)(2,1)}), (bf16[3584,256]{0,1:T(8,128)(2,1)}, bf16[256,3584]{1,0:T(8,128)(2,1)})) %all-reduce.7.cloned.1.call-update) | async-done | bytes 3670032 | tf_op jit(solution)/shard_map/psum | solution.py:51
  1511.0 0.0 copy-start.1
  1511.0 3.9 copy.11
  1515.0 0.0 copy-done.1
  1515.0 1.2 copy.15
Async XLA Ops:
  7.2 150.5 %copy-start.2 = (s32[128,256]{1,0:T(8,128)S(1)}, s32[128,256]{1,0:T(8,128)}, u32[]{:S(2)}) copy-start(s32[128,256]{1,0:T(8,128)} %param.11) | copy-start | bytes 393220
  7.2 150.5 %copy-start.4 = (f32[256]{0:T(256)S(1)}, f32[256]{0:T(256)}, u32[]{:S(2)}) copy-start(f32[256]{0:T(256)} %param.9) | copy-start | bytes 3076
  7.2 150.5 %all-gather.5.cloned.1.call-start = ((), (), s32[]{:S(2)}) async-start(), calls=%async_computation | async-start | bytes 2064384 | tf_op jit(solution)/shard_map/all_gather | solution.py:18
  7.9 226.4 %all-gather.7.cloned.1.call-start = ((), (), s32[]{:S(2)}) async-start(), calls=%async_computation.1 | async-start | bytes 2064384 | tf_op jit(solution)/shard_map/all_gather | solution.py:25
  8.7 1042.7 %all-reduce.5.cloned.1.call-start = ((), (), s32[]{:S(2)}) async-start(), calls=%async_computation.2 | async-start | bytes 3670016
  237.7 813.7 %copy-start.3 = (bf16[2,3584]{1,0:T(2,128)(2,1)S(1)}, bf16[2,3584]{1,0:T(2,128)(2,1)}, u32[]{:S(2)}) copy-start(bf16[2,3584]{1,0:T(2,128)(2,1)} %param.7) | copy-start | bytes 43012
  237.8 1273.3 %all-reduce.7.cloned.1.call-start = ((), (), s32[]{:S(2)}) async-start(), calls=%async_computation.3 | async-start | bytes 7340032 | tf_op jit(solution)/shard_map/psum | solution.py:51
  1177.2 1.9 copy-start
  1511.0 3.9 copy-start.1
Sparse Core Ops, SparseCore 0:
  11.2 117.2 all-gather.4
  131.7 102.5 all-gather.6
  237.9 813.4 all-reduce.4
  1181.5 329.4 all-reduce.6
where the time goes:
time: 1530 us; the launch traced here: 1520 us
  waiting for transfers between devices  1180 us (77%)
  blocking collectives  311 us (20%)
    unnamed x5, waiting for transfers between devices  813 us
    psum x1, waiting for transfers between devices, on_device(): lax.psum(enc_half, 'tok').astype(jnp.float32)  291 us
    all_gather x1, blocking collectives, on_device(): gathered = lax.all_gather(source, 'feat', axis=0, tiled=True)  149 us
    all_gather x1, blocking collectives, on_device(): signal_all = lax.all_gather(signal, 'feat', axis=0, tiled=True)  124 us
    all_gather x1, waiting for transfers between devices, on_device(): full_dec = lax.all_gather(dec_weight, 'tok', axis=1, tiled=True)  74.7 us
    psum x1, blocking collectives, on_device(): lax.psum(bias_part, 'tok').astype(jnp.float32)  38.3 us
  transfers between devices with their start and end apart: 4, of which 3 were waited for; matrix products, arithmetic and copies ran while one was open for 0% of the time, Pallas kernels for 0%

commit v1 on v0

v1 whole, which is shorter than its diff:
```python
import math

import jax
import jax.numpy as jnp
from jax import lax
from jax.experimental import pallas as pl
from jax.experimental.pallas import tpu as pltpu
from jax.sharding import PartitionSpec as P

BF = jnp.bfloat16
F32 = jnp.float32
W = 448


def kernel(st_ref, enc_ref, bias_ref, dec_ref, act_ref, err_ref, ge_ref, gb_ref, gd_ref,
           st_in, st_rows, S, G, wt, dt, gate, pre, feats, prnd, part, r0, r1, r2, ebuf, ss, rs):
    tok = lax.axis_index("tok")
    feat = lax.axis_index("feat")
    zh, x = tok // 4, tok % 4
    zlo, y, c = feat // 8, (feat // 2) % 4, feat % 2
    z = zh * 8 + zlo
    zq, zr = z // 4, z % 4

    def dev(x_=None, y_=None, z_=None, c_=None):
        x_ = x if x_ is None else x_
        y_ = y if y_ is None else y_
        z_ = z if z_ is None else z_
        c_ = c if c_ is None else c_
        return {"tok": (z_ // 8) * 4 + x_, "feat": ((z_ % 8) * 4 + y_) * 2 + c_}

    def tok_dev(d):
        return {"tok": (tok + d) % 8, "feat": feat}

    zoff = (1, 15, 2)
    zback = (15, 1, 14)

    barrier = pltpu.get_barrier_semaphore()
    greet = [tok_dev(d) for d in range(1, 8)]
    greet += [dev(z_=(z + 4 * d) % 16) for d in (1, 3)]
    greet += [dev(z_=(z + d) % 16) for d in zback]
    greet += [dev(y_=(y + d) % 4) for d in (1, 2, 3)]
    greet += [dev(c_=1 - c)]
    greet += [dev(z_=zh * 8 + (zlo + d) % 8) for d in range(1, 8)]
    for g in greet:
        pl.semaphore_signal(barrier, inc=1, device_id=g, device_id_type=pl.DeviceIdType.MESH)

    nxt = [0]
    sent = []

    def send(src, dst, to):
        i = nxt[0]
        nxt[0] += 1
        cp = pltpu.make_async_remote_copy(
            src_ref=src, dst_ref=dst, send_sem=ss.at[i], recv_sem=rs.at[i],
            device_id=to, device_id_type=pl.DeviceIdType.MESH)
        cp.start()
        sent.append(cp)
        return cp

    def arrive(cps):
        for cp in cps:
            cp.wait_recv()

    me = x * 2 + zh
    wt[me, 0:W, :] = enc_ref[...]
    wt[me, W:W + 128, :] = act_ref[...].astype(F32).astype(BF)
    dt[me] = dec_ref[...]
    pl.semaphore_wait(barrier, len(greet))

    ex = [send(st_ref.at[(tok + d) % 8], st_in.at[tok], tok_dev(d)) for d in range(1, 8)]
    wz = send(wt.at[me], wt.at[me], dev(z_=(z + 8) % 16))
    st_in[tok] = st_ref[tok]
    arrive(ex)
    for k in range(8):
        v = st_in[k]
        st_rows[0, 2 * k:2 * k + 2, :] = v[0:2]
        st_rows[1, 2 * k:2 * k + 2, :] = v[2:4]

    cyx = (c * 4 + y) * 4 + x
    base = cyx * 4

    def gather_z(buf):
        own = buf.at[base + zq, zr]
        arrive([send(own, own, dev(z_=(z + 4 * d) % 16)) for d in (1, 3, 2)])
        col = buf.at[pl.ds(base, 4), zr]
        arrive([send(col, col, dev(z_=(z + d) % 16)) for d in zoff])

    def gather_x(buf):
        blk = buf.at[pl.ds(base, 4)]
        return [send(blk, blk, dev(x_=(x + d) % 4)) for d in (1, 3, 2)]

    def gather_y(buf):
        blk = buf.at[pl.ds((c * 4 + y) * 16, 16)]
        return [send(blk, blk, dev(y_=(y + d) % 4)) for d in (1, 3, 2)]

    def gather_c(buf):
        blk = buf.at[pl.ds(c * 64, 64)]
        return [send(blk, blk, dev(c_=1 - c))]

    S[base + zq, zr] = st_rows[0].astype(BF)
    gather_z(S)
    sx = gather_x(S)
    arrive([wz])
    pair = wt.at[pl.ds(2 * x, 2)]
    wx = [send(pair, pair, dev(x_=(x + d) % 4)) for d in (1, 3, 2)]
    arrive(sx)
    sy = gather_y(S)
    dz = send(dt.at[me], dt.at[me], dev(z_=(z + 8) % 16))
    arrive(wx)

    for h in range(2):
        n = lax.broadcasted_iota(jnp.int32, (512, 128), 0)
        m = lax.broadcasted_iota(jnp.int32, (512, 128), 1)
        fidx = (((n // 16) % 8) * 4 + n // 128) * 2 + h
        want = fidx * 2 + n % 2
        tn = (n // 2) % 8
        acc = jnp.zeros((512, 256), F32)
        for t in range(8):
            perm = jnp.where((m == want) & (tn == t), 1.0, 0.0).astype(BF)
            acc += jnp.dot(perm, wt[(t % 4) * 2 + t // 4, W:W + 128, :], preferred_element_type=F32)
        gate[h] = acc

    def rows(buf, h, k):
        return jnp.concatenate(
            [buf[pl.ds(((h * 4 + yy) * 4 + k // 2) * 4 + (k % 2) * 2, 2)].reshape(128, W) for yy in range(4)],
            axis=0)

    def encode(h):
        pre[...] = jnp.zeros((512, 256), F32)

        def step(k, _):
            pre[...] += jnp.dot(rows(S, h, k), wt[k, 0:W, :], preferred_element_type=F32)
            return 0

        lax.fori_loop(0, 8, step, 0)
        feats[h] = (gate[h] * (pre[...] + bias_ref[...])).astype(BF)

    def decode(h):
        r = lax.dot_general(feats[h], dt[me], (((1,), (1,)), ((), ())), preferred_element_type=F32)
        part[h] = r.reshape(4, 8, 16, W)

    arrive(sy)
    sc = gather_c(S)
    encode(c)
    arrive(sc)
    encode(1 - c)
    decode(1 - c)
    pc = send(part.at[1 - c], r0, dev(c_=1 - c))
    arrive([dz])
    dpair = dt.at[pl.ds(2 * x, 2)]
    dx = [send(dpair, dpair, dev(x_=(x + d) % 4)) for d in (1, 3, 2)]
    decode(c)
    arrive([pc])
    py = []
    for d in (2, 1, 3):
        yy = (y + d) % 4
        part[c, yy] = part[c, yy] + r0[yy]
        py.append(send(part.at[c, yy], r1.at[d], dev(y_=yy)))
    arrive(py)
    part[c, y] = part[c, y] + r0[y] + r1[1] + r1[2] + r1[3]
    pz = [send(part.at[c, y, (zlo + d) % 8], r2.at[d], dev(z_=zh * 8 + (zlo + d) % 8)) for d in range(1, 8)]
    arrive(pz)
    recon = part[c, y, zlo]
    for d in range(1, 8):
        recon = recon + r2[d]
    err = recon - st_rows[1]
    G[base + zq, zr] = (err * (1.0 / 32.0)).astype(BF)
    for k in range(8):
        ebuf[k] = err[2 * k:2 * k + 2]
    err_ref[tok] = ebuf[tok]
    eo = [send(ebuf.at[(tok + d) % 8], err_ref.at[tok], tok_dev(d)) for d in range(1, 8)]
    gather_z(G)
    arrive(gather_x(G))
    gy = gather_y(G)
    arrive(dx)
    arrive(gy)
    gc = gather_c(G)

    def back(h):
        pre[...] = jnp.zeros((512, 256), F32)

        def step(k, _):
            pre[...] += jnp.dot(rows(G, h, k), dt[k], preferred_element_type=F32)
            return 0

        lax.fori_loop(0, 8, step, 0)
        g = gate[h] * pre[...]
        prnd[h] = g.astype(BF)
        return jnp.sum(g, axis=0, keepdims=True)

    b0 = back(c)
    arrive(gc)
    gb_ref[...] = b0 + back(1 - c)

    def grads(k, _):
        t = (k % 2) * 4 + k // 2
        ge = jnp.zeros((W, 256), F32)
        gd = jnp.zeros((256, W), F32)
        for h in range(2):
            ge += lax.dot_general(rows(S, h, k), prnd[h], (((0,), (0,)), ((), ())), preferred_element_type=F32)
            gd += lax.dot_general(feats[h], rows(G, h, k), (((0,), (0,)), ((), ())), preferred_element_type=F32)
        ge_ref[t] = ge.astype(BF)
        gd_ref[t] = gd.astype(BF)
        return 0

    lax.fori_loop(0, 8, grads, 0)
    arrive(eo)
    for cp in sent:
        cp.wait_send()


def on_device(source, target, enc_weight, enc_bias, dec_weight, active):
    st = jnp.concatenate([source, target], axis=0).astype(F32)
    st = st.reshape(4, 8, W).transpose(1, 0, 2)
    vm = pl.BlockSpec(memory_space=pltpu.VMEM)
    err, ge, gb, gd = pl.pallas_call(
        kernel,
        out_shape=(
            jax.ShapeDtypeStruct((8, 2, W), F32),
            jax.ShapeDtypeStruct((8, W, 256), BF),
            jax.ShapeDtypeStruct((1, 256), F32),
            jax.ShapeDtypeStruct((8, 256, W), BF),
        ),
        in_specs=[vm] * 5,
        out_specs=[vm] * 4,
        scratch_shapes=[
            pltpu.VMEM((8, 4, W), F32),
            pltpu.VMEM((2, 16, W), F32),
            pltpu.VMEM((128, 4, 16, W), BF),
            pltpu.VMEM((128, 4, 16, W), BF),
            pltpu.VMEM((8, W + 128, 256), BF),
            pltpu.VMEM((8, W, 256), BF),
            pltpu.VMEM((2, 512, 256), F32),
            pltpu.VMEM((512, 256), F32),
            pltpu.VMEM((2, 512, 256), BF),
            pltpu.VMEM((2, 512, 256), BF),
            pltpu.VMEM((2, 4, 8, 16, W), F32),
            pltpu.VMEM((4, 8, 16, W), F32),
            pltpu.VMEM((4, 8, 16, W), F32),
            pltpu.VMEM((8, 16, W), F32),
            pltpu.VMEM((8, 2, W), F32),
            pltpu.SemaphoreType.DMA((72,)),
            pltpu.SemaphoreType.DMA((72,)),
        ],
        compiler_params=pltpu.CompilerParams(
            collective_id=0, has_side_effects=True, vmem_limit_bytes=56 * 1024 * 1024),
    )(st, enc_weight, enc_bias.reshape(1, 256), dec_weight.T, active)
    err = err.transpose(1, 0, 2).reshape(2, 8 * W)
    return (err, ge.reshape(8 * W, 256), gb.reshape(256), gd.transpose(1, 0, 2).reshape(256, 8 * W))


def solution(mesh):
    placed = (
        P(("tok", "feat"), None),
        P(("tok", "feat"), None),
        P("tok", "feat"),
        P("feat"),
        P("feat", "tok"),
        P("tok", "feat"),
    )
    return jax.shard_map(
        on_device,
        mesh=mesh,
        in_specs=placed,
        out_specs=(P(("tok", "feat"), None), P(None, "feat"), P("feat"), P("feat", None)),
        check_vma=False,
    )
```

time: 1530 us -> 262 us (0.17)
  waiting for transfers between devices: 1180 us -> 0 us
  blocking collectives: 311 us -> 0 us
  Pallas kernels: 0 us -> 246 us
    unnamed x5 -> x0, waiting for transfers between devices: 813 us -> none
    psum x1 -> x0, waiting for transfers between devices: 291 us -> none  [on_device(): lax.psum(enc_half, 'tok').astype(jnp.float32)]
    all_gather x2 -> x0, blocking collectives: 272 us -> none  [the longest x1 149 us: on_device(): gathered = lax.all_gather(source, 'feat', axis=0, tiled=True)]
    pallas_call x0 -> x1, Pallas kernels: none -> 246 us  [on_device(): pl.pallas_call(kernel, out_shape=(jax.ShapeDtypeStruct((8, 2, W), F32), j...]
    all_gather x2 -> x0, waiting for transfers between devices: 74.7 us -> none  [the longest x1 74.7 us: on_device(): full_dec = lax.all_gather(dec_weight, 'tok', axis=1, tiled=True)]
    psum x1 -> x0, blocking collectives: 38.3 us -> none  [on_device(): lax.psum(bias_part, 'tok').astype(jnp.float32)]
  transfers between devices with their start and end apart: 4 -> 0, of which waited for: 3 -> 0; matrix products, arithmetic and copies ran while one was open for 0% -> 0% of each run, Pallas kernels for 0% -> 0%
where the time goes in v1:
time: 262 us; the launch traced here: 260 us
  Pallas kernels  246 us (94%)
  local copies, waits for them, and re-layouts  12.4 us (5%)
    pallas_call x1, Pallas kernels, on_device(): pl.pallas_call(kernel, out_shape=(jax.ShapeDtypeStruct((8, 2, W), F32), j...  246 us
    unnamed x5, local copies, waits for them, and re-layouts  5.98 us

profile of v1, /device:TPU:1, one launch (start us, length us, event | category | flops | bytes accessed | tf_op | source)
XLA Modules:
  0.0 259.9 jit_solution(551567543408575758)
XLA Ops:
  0.6 0.8 concatenate.8
  1.5 0.8 concatenate.9
  2.3 0.7 convert_bitcast_fusion.st_ref
  3.0 246.2 %shard_map.93 = (f32[8,2,448]{2,1,0:T(2,128)}, bf16[8,448,256]{2,1,0:T(8,128)(2,1)}, f32[1,256]{1,0:T(1,128)}, bf16[8,256,448]{2,1,0:T(8,128)(2,1)}) custom-call(f32[8,4,448]{2,1,0:T(4,128)} %convert_bitcast_fusion.st_ref, bf16[448,256]{1,0:T(8,128)(2,1)} %enc_ref.1, f32[1,256]{1,0:T(1,128)} %bitcast.14, bf16[448,256]{1,0:T(8,128)(2,1)} %bitcast.12, ...), custom_call_target="tpu_custom_call" | custom-call | tf_op jit(solution)/shard_map/pallas_call | solution.py:216
  249.1 0.8 copy.12
  249.9 0.7 reshape.27
  250.6 3.3 %copy.13 = bf16[256,8,448]{0,2,1:T(8,128)(2,1)S(1)} copy(bf16[256,8,448]{2,0,1:T(8,128)(2,1)} %bitcast.10) | data formatting | bytes 3670016 | tf_op jit(solution)/shard_map/transpose | solution.py:249
  253.9 2.6 copy.14
  256.4 0.0 copy-start
  256.5 2.8 %copy.17 = bf16[3584,256]{1,0:T(8,128)(2,1)} copy(bf16[3584,256]{1,0:T(8,128)(2,1)} %bitcast.11) | data formatting | bytes 3670016
  259.3 0.0 copy-done
  259.3 0.6 copy.18
  (2 shorter events, 0.0 us)
Async XLA Ops:
  256.4 2.9 %copy-start = (f32[1,256]{1,0:T(1,128)S(1)}, f32[1,256]{1,0:T(1,128)}, u32[]{:S(2)}) copy-start(f32[1,256]{1,0:T(1,128)} %get-tuple-element.10) | copy-start | bytes 3076

commit v2 on v1

v2 whole, which is shorter than its diff:
```python
import math

import jax
import jax.numpy as jnp
from jax import lax
from jax.experimental import pallas as pl
from jax.experimental.pallas import tpu as pltpu
from jax.sharding import PartitionSpec as P

BF = jnp.bfloat16
F32 = jnp.float32
W = 448


def kernel(st_ref, enc_ref, bias_ref, dec_ref, act_ref, err_ref, ge_ref, gb_ref, gd_ref,
           st_in, st_rows, S, G, ST, wt, dt, gate, pre, feats, fT, prnd, part, r0, pb, r1, qb, r2, ebuf, ss, rs):
    tok = lax.axis_index("tok")
    feat = lax.axis_index("feat")
    zh, x = tok // 4, tok % 4
    zlo, y, c = feat // 8, (feat // 2) % 4, feat % 2
    z = zh * 8 + zlo
    zq, zr = z // 4, z % 4

    def dev(x_=None, y_=None, z_=None, c_=None):
        x_ = x if x_ is None else x_
        y_ = y if y_ is None else y_
        z_ = z if z_ is None else z_
        c_ = c if c_ is None else c_
        return {"tok": (z_ // 8) * 4 + x_, "feat": ((z_ % 8) * 4 + y_) * 2 + c_}

    def tok_dev(d):
        return {"tok": (tok + d) % 8, "feat": feat}

    zoff = (1, 15, 2)
    zback = (15, 1, 14)

    barrier = pltpu.get_barrier_semaphore()
    greet = [tok_dev(d) for d in range(1, 8)]
    greet += [dev(z_=(z + 4 * d) % 16) for d in (1, 3)]
    greet += [dev(z_=(z + d) % 16) for d in zback]
    greet += [dev(y_=(y + d) % 4) for d in (1, 2, 3)]
    greet += [dev(c_=1 - c)]
    greet += [dev(z_=zh * 8 + (zlo + d) % 8) for d in range(1, 8)]
    for g in greet:
        pl.semaphore_signal(barrier, inc=1, device_id=g, device_id_type=pl.DeviceIdType.MESH)

    nxt = [0]
    sent = []

    def send(src, dst, to):
        i = nxt[0]
        nxt[0] += 1
        cp = pltpu.make_async_remote_copy(
            src_ref=src, dst_ref=dst, send_sem=ss.at[i], recv_sem=rs.at[i],
            device_id=to, device_id_type=pl.DeviceIdType.MESH)
        cp.start()
        sent.append(cp)
        return cp

    def arrive(cps):
        for cp in cps:
            cp.wait_recv()

    me = x * 2 + zh
    wt[me, 0:W, :] = enc_ref[...]
    wt[me, W:W + 128, :] = act_ref[...].astype(F32).astype(BF)
    dt[me] = dec_ref[...]
    pl.semaphore_wait(barrier, len(greet))

    ex = [send(st_ref.at[(tok + d) % 8], st_in.at[tok], tok_dev(d)) for d in range(1, 8)]
    wz = send(wt.at[me], wt.at[me], dev(z_=(z + 8) % 16))
    st_in[tok] = st_ref[tok]
    arrive(ex)
    for k in range(8):
        v = st_in[k]
        st_rows[0, 2 * k:2 * k + 2, :] = v[0:2]
        st_rows[1, 2 * k:2 * k + 2, :] = v[2:4]

    base = ((c * 4 + y) * 4 + x) * 4

    def ring_start(piece, axis):
        p = {"x_": x, "y_": y}[axis]
        fwd, bwd = dev(**{axis: (p + 1) % 4}), dev(**{axis: (p + 3) % 4})
        own = [piece(p, 0), piece(p, 1)]
        a = send(own[0], own[0], fwd)
        b = send(own[1], own[1], bwd)
        late = [send(own[1], own[1], fwd), send(own[0], own[0], bwd)]
        return piece, p, fwd, bwd, a, b, late

    def ring_pass(state):
        piece, p, fwd, bwd, a, b, late = state
        arrive([a])
        left = piece((p + 3) % 4, 0)
        f = send(left, left, fwd)
        arrive([b])
        right = piece((p + 1) % 4, 1)
        g = send(right, right, bwd)
        return late, [f, g]

    def s_piece(yy, half):
        return S.at[pl.ds((c * 4 + yy) * 16 + half * 8, 8)]

    def w_piece(buf):
        return lambda xx, half: buf.at[2 * xx + half]

    own = base + zq
    S[own, zr] = st_rows[0].astype(BF)
    arrive([send(S.at[own, zr], S.at[own, zr], dev(z_=(z + 4 * d) % 16)) for d in (2, 1, 3)])
    col = S.at[pl.ds(base, 4), zr]
    arrive([send(col, col, dev(z_=(z + d) % 16)) for d in zoff])
    blk = S.at[pl.ds(base, 4)]
    sx = [send(blk, blk, dev(x_=(x + d) % 4)) for d in (1, 3, 2)]
    arrive([wz])
    wx = ring_start(w_piece(wt), "x_")
    dz = send(dt.at[me], dt.at[me], dev(z_=(z + 8) % 16))
    arrive(sx)
    sy = ring_start(s_piece, "y_")

    def s_swap(yy):
        q = S.at[pl.ds((c * 4 + yy) * 16, 16)]
        return send(q, q, dev(c_=1 - c))

    sc = [s_swap(y)]
    wl, wf = ring_pass(wx)
    sl, sf = ring_pass(sy)
    arrive(wl)
    arrive(wf)

    for h in range(2):
        n = lax.broadcasted_iota(jnp.int32, (512, 128), 0)
        m = lax.broadcasted_iota(jnp.int32, (512, 128), 1)
        fidx = (((n // 16) % 8) * 4 + n // 128) * 2 + h
        want = fidx * 2 + n % 2
        tn = (n // 2) % 8
        acc = jnp.zeros((512, 256), F32)
        for t in range(8):
            perm = jnp.where((m == want) & (tn == t), 1.0, 0.0).astype(BF)
            acc += jnp.dot(perm, wt[(t % 4) * 2 + t // 4, W:W + 128, :], preferred_element_type=F32)
        gate[h] = acc

    def rows(h, k):
        return jnp.concatenate(
            [S[pl.ds(((h * 4 + yy) * 4 + k // 2) * 4 + (k % 2) * 2, 2)].reshape(128, W) for yy in range(4)],
            axis=0)

    def g_rows(h, k):
        parts = []
        for yy in range(4):
            parts.append(G[0, ((h * 4 + yy) * 4 + k // 2) * 2 + k % 2].reshape(64, W))
            parts.append(G[1, ((h * 4 + k // 2) * 4 + yy) * 2 + k % 2].reshape(64, W))
        return jnp.concatenate(parts, axis=0)

    def encode(h):
        pre[...] = jnp.zeros((512, 256), F32)

        def step(k, _):
            pre[...] += jnp.dot(rows(h, k), wt[k, 0:W, :], preferred_element_type=F32)
            return 0

        lax.fori_loop(0, 8, step, 0)
        feats[h] = (gate[h] * (pre[...] + bias_ref[...])).astype(BF)

    def decode(h):
        r = lax.dot_general(feats[h], dt[me], (((1,), (1,)), ((), ())), preferred_element_type=F32)
        part[h] = r.reshape(4, 8, 16, W)

    arrive(sl)
    sc += [s_swap((y + 1) % 4), s_swap((y + 3) % 4)]
    arrive(sf)
    sc.append(s_swap((y + 2) % 4))
    encode(c)
    arrive(sc)
    encode(1 - c)
    decode(1 - c)
    pc = [send(part.at[1 - c, (y + d) % 4], r0.at[(y + d) % 4], dev(c_=1 - c)) for d in (2, 1, 3, 0)]
    decode(c)
    arrive([dz])
    dx = ring_start(w_piece(dt), "x_")
    py = []
    for i, d in enumerate((2, 1, 3)):
        yy = (y + d) % 4
        arrive([pc[i]])
        pb[yy] = (part[c, yy] + r0[yy]).astype(BF)
        py.append(send(pb.at[yy], r1.at[d], dev(y_=yy)))
    arrive([pc[3]])
    for h in range(2):
        fT[h] = feats[h].T
    arrive(py)
    total = part[c, y] + r0[y] + r1[1].astype(F32) + r1[2].astype(F32) + r1[3].astype(F32)
    part[c, y] = total
    qb[...] = total.astype(BF)
    pz = [send(qb.at[(zlo + d) % 8], r2.at[d], dev(z_=zh * 8 + (zlo + d) % 8)) for d in (4, 3, 5, 2, 6, 1, 7)]
    dl, df = ring_pass(dx)
    arrive(pz)
    recon = part[c, y, zlo]
    for d in range(1, 8):
        recon = recon + r2[d].astype(F32)
    err = recon - st_rows[1]

    zl = zq % 2
    b0 = ((c * 4 + y) * 4 + x) * 2
    b1 = ((c * 4 + x) * 4 + y) * 2
    gi = b0 + zl * (b1 - b0) + zh
    G[zl, gi, zr] = (err * (1.0 / 32.0)).astype(BF)
    gown = G.at[zl, gi, zr]
    gz = [send(gown, gown, dev(z_=(z + 4 * d) % 16)) for d in (2, 1, 3)]
    for k in range(8):
        ebuf[k] = err[2 * k:2 * k + 2]
    err_ref[tok] = ebuf[tok]
    eo = [send(ebuf.at[(tok + d) % 8], err_ref.at[tok], tok_dev(d)) for d in range(1, 8)]
    arrive(gz)
    cols = [G.at[0, pl.ds(b0, 2), zr], G.at[1, pl.ds(b1, 2), zr]]
    arrive([send(q, q, dev(z_=(z + d) % 16)) for d in zoff for q in cols])
    g0, g1 = G.at[0, pl.ds(b0, 2)], G.at[1, pl.ds(b1, 2)]
    one = []
    for d in (1, 3, 2):
        one.append(send(g0, g0, dev(x_=(x + d) % 4)))
        one.append(send(g1, g1, dev(y_=(y + d) % 4)))
    arrive(one)

    def g_piece(half_no):
        return lambda p, half: G.at[half_no, pl.ds((c * 4 + p) * 8 + half * 4, 4)]

    def g_swap(half_no, p):
        q = G.at[half_no, pl.ds((c * 4 + p) * 8, 8)]
        return send(q, q, dev(c_=1 - c))

    ra = ring_start(g_piece(0), "y_")
    rb = ring_start(g_piece(1), "x_")
    gc = [g_swap(0, y), g_swap(1, x)]

    def turn(k, _):
        ST[k] = jnp.concatenate([rows(0, k), rows(1, k)], axis=0).T
        return 0

    lax.fori_loop(0, 4, turn, 0)
    al, af = ring_pass(ra)
    bl, bf = ring_pass(rb)
    arrive(dl)
    arrive(df)
    arrive(al)
    arrive(bl)
    gc += [g_swap(0, (y + 1) % 4), g_swap(0, (y + 3) % 4), g_swap(1, (x + 1) % 4), g_swap(1, (x + 3) % 4)]
    lax.fori_loop(4, 8, turn, 0)
    arrive(af)
    gc.append(g_swap(0, (y + 2) % 4))
    arrive(bf)
    gc.append(g_swap(1, (x + 2) % 4))

    def back(h):
        pre[...] = jnp.zeros((512, 256), F32)

        def step(k, _):
            pre[...] += jnp.dot(g_rows(h, k), dt[k], preferred_element_type=F32)
            return 0

        lax.fori_loop(0, 8, step, 0)
        g = gate[h] * pre[...]
        prnd[h] = g.astype(BF)
        return jnp.sum(g, axis=0, keepdims=True)

    bsum = back(c)
    arrive(gc)
    gb_ref[...] = bsum + back(1 - c)

    def grads(n, _):
        halves = []
        for odd in range(2):
            t = 2 * n + odd
            k = (t % 4) * 2 + t // 4
            ge = jnp.zeros((W, 256), F32)
            gd = jnp.zeros((256, W), F32)
            for h in range(2):
                ge += jnp.dot(ST[k, :, h * 512:h * 512 + 512], prnd[h], preferred_element_type=F32)
                gd += jnp.dot(fT[h], g_rows(h, k), preferred_element_type=F32)
            ge_ref[pl.ds(pl.multiple_of(t * W, W), W), :] = ge.astype(BF)
            halves.append(gd)
        both = jnp.concatenate(halves, axis=1).astype(BF)
        gd_ref[:, pl.ds(pl.multiple_of(n * 2 * W, 2 * W), 2 * W)] = both
        return 0

    lax.fori_loop(0, 4, grads, 0)
    arrive(eo)
    for cp in sent:
        cp.wait_send()


def on_device(source, target, enc_weight, enc_bias, dec_weight, active):
    st = jnp.concatenate([source, target], axis=0).astype(F32)
    st = st.reshape(4, 8, W).transpose(1, 0, 2)
    vm = pl.BlockSpec(memory_space=pltpu.VMEM)
    err, ge, gb, gd = pl.pallas_call(
        kernel,
        out_shape=(
            jax.ShapeDtypeStruct((8, 2, W), F32),
            jax.ShapeDtypeStruct((8 * W, 256), BF),
            jax.ShapeDtypeStruct((1, 256), F32),
            jax.ShapeDtypeStruct((256, 8 * W), BF),
        ),
        in_specs=[vm] * 5,
        out_specs=[vm] * 4,
        scratch_shapes=[
            pltpu.VMEM((8, 4, W), F32),
            pltpu.VMEM((2, 16, W), F32),
            pltpu.VMEM((128, 4, 16, W), BF),
            pltpu.VMEM((2, 64, 4, 16, W), BF),
            pltpu.VMEM((8, W, 1024), BF),
            pltpu.VMEM((8, W + 128, 256), BF),
            pltpu.VMEM((8, W, 256), BF),
            pltpu.VMEM((2, 512, 256), F32),
            pltpu.VMEM((512, 256), F32),
            pltpu.VMEM((2, 512, 256), BF),
            pltpu.VMEM((2, 256, 512), BF),
            pltpu.VMEM((2, 512, 256), BF),
            pltpu.VMEM((2, 4, 8, 16, W), F32),
            pltpu.VMEM((4, 8, 16, W), F32),
            pltpu.VMEM((4, 8, 16, W), BF),
            pltpu.VMEM((4, 8, 16, W), BF),
            pltpu.VMEM((8, 16, W), BF),
            pltpu.VMEM((8, 16, W), BF),
            pltpu.VMEM((8, 2, W), F32),
            pltpu.SemaphoreType.DMA((128,)),
            pltpu.SemaphoreType.DMA((128,)),
        ],
        compiler_params=pltpu.CompilerParams(
            collective_id=0, has_side_effects=True, vmem_limit_bytes=56 * 1024 * 1024),
    )(st, enc_weight, enc_bias.reshape(1, 256), dec_weight.T, active)
    err = err.transpose(1, 0, 2).reshape(2, 8 * W)
    return (err, ge, gb.reshape(256), gd)


def solution(mesh):
    placed = (
        P(("tok", "feat"), None),
        P(("tok", "feat"), None),
        P("tok", "feat"),
        P("feat"),
        P("feat", "tok"),
        P("tok", "feat"),
    )
    return jax.shard_map(
        on_device,
        mesh=mesh,
        in_specs=placed,
        out_specs=(P(("tok", "feat"), None), P(None, "feat"), P("feat"), P("feat", None)),
        check_vma=False,
    )
```

time: 262 us -> 199 us (0.76)
  Pallas kernels: 246 us -> 190 us
  local copies, waits for them, and re-layouts: 12.4 us -> 7.89 us
    pallas_call x1, Pallas kernels: 246 us -> 190 us  [on_device(): pl.pallas_call(kernel, out_shape=(jax.ShapeDtypeStruct((8, 2, W), F32), j...]
    transpose x1 -> x0, local copies, waits for them, and re-layouts: 3.27 us -> none  [on_device(): gd.transpose(1, 0, 2).reshape(256, 8 * W)]
    unnamed x5 -> x7, local copies, waits for them, and re-layouts: 5.98 us -> 4.78 us
where the time goes in v2:
time: 199 us
  Pallas kernels  190 us (95%)
  local copies, waits for them, and re-layouts  7.89 us (4%)
    pallas_call x1, Pallas kernels, on_device(): pl.pallas_call(kernel, out_shape=(jax.ShapeDtypeStruct((8, 2, W), F32), j...  190 us
    unnamed x7, local copies, waits for them, and re-layouts  4.78 us

profile of v2, /device:TPU:1, one launch (start us, length us, event | category | flops | bytes accessed | tf_op | source)
XLA Modules:
  0.0 198.8 jit_solution(759373959261222978)
XLA Ops:
  0.6 0.8 concatenate.8
  1.5 0.8 concatenate.9
  2.3 0.7 convert_bitcast_fusion.st_ref
  3.0 189.6 %shard_map.93 = (f32[8,2,448]{2,1,0:T(2,128)}, bf16[3584,256]{1,0:T(8,128)(2,1)}, f32[1,256]{1,0:T(1,128)}, bf16[256,3584]{1,0:T(8,128)(2,1)}) custom-call(f32[8,4,448]{2,1,0:T(4,128)} %convert_bitcast_fusion.st_ref, bf16[448,256]{1,0:T(8,128)(2,1)} %enc_ref.1, f32[1,256]{1,0:T(1,128)} %bitcast.8, bf16[448,256]{1,0:T(8,128)(2,1)} %bitcast.6, s32[128,256]{1,0:T(8,128)} %act_ref.1), custom_call_target="tpu_custom_call" | custom-call | tf_op jit(solution)/shard_map/pallas_call | solution.py:292
  192.6 0.8 copy.12
  193.3 0.7 reshape.21
  194.0 0.0 copy-start.1
  194.0 0.0 copy-start
  194.0 3.0 %copy.16 = bf16[3584,256]{1,0:T(8,128)(2,1)} copy(bf16[3584,256]{1,0:T(8,128)(2,1)} %get-tuple-element.17) | data formatting | bytes 3670016
  197.0 0.0 copy-done.1
  197.0 0.6 copy.17
  197.6 0.0 copy-done
  197.6 1.2 copy.18
  (2 shorter events, 0.0 us)
Async XLA Ops:
  194.0 3.0 %copy-start.1 = (f32[1,256]{1,0:T(1,128)S(1)}, f32[1,256]{1,0:T(1,128)}, u32[]{:S(2)}) copy-start(f32[1,256]{1,0:T(1,128)} %get-tuple-element.10) | copy-start | bytes 3076
  194.0 3.6 %copy-start = (bf16[256,3584]{1,0:T(8,128)(2,1)S(1)}, bf16[256,3584]{1,0:T(8,128)(2,1)}, u32[]{:S(2)}) copy-start(bf16[256,3584]{1,0:T(8,128)(2,1)} %get-tuple-element.19) | copy-start | bytes 5505028

commit v3 on v2

v3 whole, which is shorter than its diff:
```python
import math

import jax
import jax.numpy as jnp
from jax import lax
from jax.experimental import pallas as pl
from jax.experimental.pallas import tpu as pltpu
from jax.sharding import PartitionSpec as P

BF = jnp.bfloat16
F32 = jnp.float32
W = 448


def kernel(src_ref, tgt_ref, enc_ref, bias_ref, dec_ref, act_ref, err_ref, ge_ref, gb_ref, gd_ref,
           st_ref, st_in, st_rows, err_in, S, G, ST, at, wt, dt, gate, pre, feats, fT, prnd, part, r0, pb, r1, qb, r2, ebuf, ss, rs):
    tok = lax.axis_index("tok")
    feat = lax.axis_index("feat")
    zh, x = tok // 4, tok % 4
    zlo, y, c = feat // 8, (feat // 2) % 4, feat % 2
    z = zh * 8 + zlo
    zq, zr = z // 4, z % 4

    def dev(x_=None, y_=None, z_=None, c_=None):
        x_ = x if x_ is None else x_
        y_ = y if y_ is None else y_
        z_ = z if z_ is None else z_
        c_ = c if c_ is None else c_
        return {"tok": (z_ // 8) * 4 + x_, "feat": ((z_ % 8) * 4 + y_) * 2 + c_}

    def tok_dev(d):
        return {"tok": (tok + d) % 8, "feat": feat}

    zoff = (1, 15, 2)
    zback = (15, 1, 14)

    barrier = pltpu.get_barrier_semaphore()
    greet = [tok_dev(d) for d in range(1, 8)]
    greet += [dev(z_=(z + 4 * d) % 16) for d in (1, 3)]
    greet += [dev(z_=(z + d) % 16) for d in zback]
    greet += [dev(y_=(y + d) % 4) for d in (1, 2, 3)]
    greet += [dev(c_=1 - c)]
    greet += [dev(z_=zh * 8 + (zlo + d) % 8) for d in range(1, 8)]
    for g in greet:
        pl.semaphore_signal(barrier, inc=1, device_id=g, device_id_type=pl.DeviceIdType.MESH)

    nxt = [0]
    sent = []

    def send(src, dst, to):
        i = nxt[0]
        nxt[0] += 1
        cp = pltpu.make_async_remote_copy(
            src_ref=src, dst_ref=dst, send_sem=ss.at[i], recv_sem=rs.at[i],
            device_id=to, device_id_type=pl.DeviceIdType.MESH)
        cp.start()
        sent.append(cp)
        return cp

    def arrive(cps):
        for cp in cps:
            cp.wait_recv()

    me = x * 2 + zh
    across = dev(z_=(z + 8) % 16)
    wt[me] = enc_ref[...]
    at[me] = act_ref[...].astype(F32).astype(BF)
    dt[me] = dec_ref[...]
    rows_in = jnp.concatenate([src_ref[...].astype(F32), tgt_ref[...].astype(F32)], axis=0)
    for k in range(8):
        st_ref[k] = rows_in[:, k * W:k * W + W]
    pl.semaphore_wait(barrier, len(greet))

    def ring_start(piece, axis):
        p = {"x_": x, "y_": y}[axis]
        fwd, bwd = dev(**{axis: (p + 1) % 4}), dev(**{axis: (p + 3) % 4})
        own = [piece(p, 0), piece(p, 1)]
        a = send(own[0], own[0], fwd)
        b = send(own[1], own[1], bwd)
        late = [send(own[1], own[1], fwd), send(own[0], own[0], bwd)]
        return piece, p, fwd, bwd, a, b, late

    def ring_pass(state):
        piece, p, fwd, bwd, a, b, late = state
        arrive([a])
        left = piece((p + 3) % 4, 0)
        f = send(left, left, fwd)
        arrive([b])
        right = piece((p + 1) % 4, 1)
        g = send(right, right, bwd)
        return late, [f, g]

    def w_piece(buf, side):
        return lambda xx, half: buf.at[2 * xx + side, pl.ds(half * (W // 2), W // 2)]

    zl = zq % 2
    b0 = ((c * 4 + y) * 4 + x) * 2
    b1 = ((c * 4 + x) * 4 + y) * 2
    gi = b0 + zl * (b1 - b0) + zh

    def far(buf):
        own = buf.at[zl, gi, zr]
        return [send(own, own, dev(z_=(z + 4 * d) % 16)) for d in (2, 1, 3)]

    def near(buf):
        cols = [buf.at[0, pl.ds(b0, 2), zr], buf.at[1, pl.ds(b1, 2), zr]]
        return [send(q, q, dev(z_=(z + d) % 16)) for d in zoff for q in cols]

    def light(buf):
        q0, q1 = buf.at[0, pl.ds(b0, 2)], buf.at[1, pl.ds(b1, 2)]
        out = []
        for d in (1, 3, 2):
            out.append(send(q0, q0, dev(x_=(x + d) % 4)))
            out.append(send(q1, q1, dev(y_=(y + d) % 4)))
        return out

    def heavy(buf, half_no):
        return lambda p, half: buf.at[half_no, pl.ds((c * 4 + p) * 8 + half * 4, 4)]

    def swap(buf, half_no, p):
        q = buf.at[half_no, pl.ds((c * 4 + p) * 8, 8)]
        return send(q, q, dev(c_=1 - c))

    ex = [send(st_ref.at[(tok + d) % 8], st_in.at[tok], tok_dev(d)) for d in range(1, 8)]
    az = send(at.at[me], at.at[me], across)
    w0 = ring_start(w_piece(wt, zh), "x_")

    def w_part(i):
        q = wt.at[me, pl.ds(i * (W // 4), W // 4)]
        return send(q, q, across)

    st_in[tok] = st_ref[tok]
    arrive(ex)
    for k in range(8):
        v = st_in[k]
        st_rows[0, 2 * k:2 * k + 2, :] = v[0:2]
        st_rows[1, 2 * k:2 * k + 2, :] = v[2:4]
    S[zl, gi, zr] = st_rows[0].astype(BF)
    sz = far(S)
    wz = [w_part(0)]
    arrive(sz)
    sn = near(S)
    w0l, w0f = ring_pass(w0)
    arrive(sn)
    one = light(S)
    wz += [w_part(1), w_part(2), w_part(3)]
    arrive([az])
    apair = at.at[pl.ds(2 * x, 2)]
    ax = [send(apair, apair, dev(x_=(x + d) % 4)) for d in (1, 3, 2)]
    arrive(one)
    ra = ring_start(heavy(S, 0), "y_")
    rb = ring_start(heavy(S, 1), "x_")
    sc = [swap(S, 0, y), swap(S, 1, x)]
    arrive(w0l)
    arrive(w0f)
    al, af = ring_pass(ra)
    bl, bf = ring_pass(rb)
    arrive(wz)
    w1 = ring_start(w_piece(wt, 1 - zh), "x_")
    dz = send(dt.at[me], dt.at[me], across)
    arrive(ax)

    for h in range(2):
        n = lax.broadcasted_iota(jnp.int32, (512, 128), 0)
        m = lax.broadcasted_iota(jnp.int32, (512, 128), 1)
        fidx = (((n // 16) % 8) * 4 + n // 128) * 2 + h
        want = fidx * 2 + n % 2
        tn = (n // 2) % 8
        acc = jnp.zeros((512, 256), F32)
        for t in range(8):
            perm = jnp.where((m == want) & (tn == t), 1.0, 0.0).astype(BF)
            acc += jnp.dot(perm, at[(t % 4) * 2 + t // 4], preferred_element_type=F32)
        gate[h] = acc

    w1l, w1f = ring_pass(w1)
    d0 = ring_start(w_piece(dt, zh), "x_")

    def rows(buf, h, k):
        parts = []
        for yy in range(4):
            parts.append(buf[0, ((h * 4 + yy) * 4 + k // 2) * 2 + k % 2].reshape(64, W))
            parts.append(buf[1, ((h * 4 + k // 2) * 4 + yy) * 2 + k % 2].reshape(64, W))
        return jnp.concatenate(parts, axis=0)

    def encode(h):
        pre[...] = jnp.zeros((512, 256), F32)

        def step(k, _):
            pre[...] += jnp.dot(rows(S, h, k), wt[k], preferred_element_type=F32)
            return 0

        lax.fori_loop(0, 8, step, 0)
        feats[h] = (gate[h] * (pre[...] + bias_ref[...])).astype(BF)

    def decode(h):
        r = lax.dot_general(feats[h], dt[me], (((1,), (1,)), ((), ())), preferred_element_type=F32)
        part[h] = r.reshape(4, 8, 16, W)

    arrive(al)
    arrive(bl)
    sc += [swap(S, 0, (y + 1) % 4), swap(S, 0, (y + 3) % 4), swap(S, 1, (x + 1) % 4), swap(S, 1, (x + 3) % 4)]
    arrive(af)
    sc.append(swap(S, 0, (y + 2) % 4))
    arrive(bf)
    sc.append(swap(S, 1, (x + 2) % 4))
    arrive(w1l)
    arrive(w1f)
    encode(c)
    d0l, d0f = ring_pass(d0)
    arrive(sc)
    encode(1 - c)
    decode(1 - c)
    pc = [send(part.at[1 - c, (y + d) % 4], r0.at[(y + d) % 4], dev(c_=1 - c)) for d in (2, 1, 3, 0)]
    decode(c)
    arrive([dz])
    d1 = ring_start(w_piece(dt, 1 - zh), "x_")
    py = []
    for i, d in enumerate((2, 1, 3)):
        yy = (y + d) % 4
        arrive([pc[i]])
        pb[yy] = (part[c, yy] + r0[yy]).astype(BF)
        py.append(send(pb.at[yy], r1.at[d], dev(y_=yy)))
    arrive([pc[3]])
    for h in range(2):
        fT[h] = feats[h].T
    arrive(py)
    total = part[c, y] + r0[y] + r1[1].astype(F32) + r1[2].astype(F32) + r1[3].astype(F32)
    part[c, y] = total
    qb[...] = total.astype(BF)
    pz = [send(qb.at[(zlo + d) % 8], r2.at[d], dev(z_=zh * 8 + (zlo + d) % 8)) for d in (4, 3, 5, 2, 6, 1, 7)]
    d1l, d1f = ring_pass(d1)
    arrive(pz)
    recon = part[c, y, zlo]
    for d in range(1, 8):
        recon = recon + r2[d].astype(F32)
    err = recon - st_rows[1]

    G[zl, gi, zr] = (err * (1.0 / 32.0)).astype(BF)
    gz = far(G)
    for k in range(8):
        ebuf[k] = err[2 * k:2 * k + 2]
    err_in[tok] = ebuf[tok]
    eo = [send(ebuf.at[(tok + d) % 8], err_in.at[tok], tok_dev(d)) for d in range(1, 8)]
    arrive(gz)
    arrive(near(G))
    arrive(light(G))
    ra = ring_start(heavy(G, 0), "y_")
    rb = ring_start(heavy(G, 1), "x_")
    gc = [swap(G, 0, y), swap(G, 1, x)]

    def turn(k, _):
        ST[k] = jnp.concatenate([rows(S, 0, k), rows(S, 1, k)], axis=0).T
        return 0

    lax.fori_loop(0, 4, turn, 0)
    al, af = ring_pass(ra)
    bl, bf = ring_pass(rb)
    for cps in (d0l, d0f, d1l, d1f):
        arrive(cps)
    arrive(al)
    arrive(bl)
    gc += [swap(G, 0, (y + 1) % 4), swap(G, 0, (y + 3) % 4), swap(G, 1, (x + 1) % 4), swap(G, 1, (x + 3) % 4)]
    lax.fori_loop(4, 8, turn, 0)
    arrive(af)
    gc.append(swap(G, 0, (y + 2) % 4))
    arrive(bf)
    gc.append(swap(G, 1, (x + 2) % 4))

    def back(h):
        pre[...] = jnp.zeros((512, 256), F32)

        def step(k, _):
            pre[...] += jnp.dot(rows(G, h, k), dt[k], preferred_element_type=F32)
            return 0

        lax.fori_loop(0, 8, step, 0)
        g = gate[h] * pre[...]
        prnd[h] = g.astype(BF)
        return jnp.sum(g, axis=0, keepdims=True)

    bsum = back(c)
    arrive(gc)
    gb_ref[...] = bsum + back(1 - c)

    def grads(n, _):
        halves = []
        for odd in range(2):
            t = 2 * n + odd
            k = (t % 4) * 2 + t // 4
            ge = jnp.zeros((W, 256), F32)
            gd = jnp.zeros((256, W), F32)
            for h in range(2):
                ge += jnp.dot(ST[k, :, h * 512:h * 512 + 512], prnd[h], preferred_element_type=F32)
                gd += jnp.dot(fT[h], rows(G, h, k), preferred_element_type=F32)
            ge_ref[pl.ds(pl.multiple_of(t * W, W), W), :] = ge.astype(BF)
            halves.append(gd)
        both = jnp.concatenate(halves, axis=1).astype(BF)
        gd_ref[:, pl.ds(pl.multiple_of(n * 2 * W, 2 * W), 2 * W)] = both
        return 0

    arrive(eo)
    err_ref[...] = jnp.concatenate([err_in[k] for k in range(8)], axis=1)
    lax.fori_loop(0, 4, grads, 0)
    for cp in sent:
        cp.wait_send()


def on_device(source, target, enc_weight, enc_bias, dec_weight, active):
    vm = pl.BlockSpec(memory_space=pltpu.VMEM)
    err, ge, gb, gd = pl.pallas_call(
        kernel,
        out_shape=(
            jax.ShapeDtypeStruct((2, 8 * W), F32),
            jax.ShapeDtypeStruct((8 * W, 256), BF),
            jax.ShapeDtypeStruct((1, 256), F32),
            jax.ShapeDtypeStruct((256, 8 * W), BF),
        ),
        in_specs=[vm] * 6,
        out_specs=[vm] * 4,
        scratch_shapes=[
            pltpu.VMEM((8, 4, W), F32),
            pltpu.VMEM((8, 4, W), F32),
            pltpu.VMEM((2, 16, W), F32),
            pltpu.VMEM((8, 2, W), F32),
            pltpu.VMEM((2, 64, 4, 16, W), BF),
            pltpu.VMEM((2, 64, 4, 16, W), BF),
            pltpu.VMEM((8, W, 1024), BF),
            pltpu.VMEM((8, 128, 256), BF),
            pltpu.VMEM((8, W, 256), BF),
            pltpu.VMEM((8, W, 256), BF),
            pltpu.VMEM((2, 512, 256), F32),
            pltpu.VMEM((512, 256), F32),
            pltpu.VMEM((2, 512, 256), BF),
            pltpu.VMEM((2, 256, 512), BF),
            pltpu.VMEM((2, 512, 256), BF),
            pltpu.VMEM((2, 4, 8, 16, W), F32),
            pltpu.VMEM((4, 8, 16, W), F32),
            pltpu.VMEM((4, 8, 16, W), BF),
            pltpu.VMEM((4, 8, 16, W), BF),
            pltpu.VMEM((8, 16, W), BF),
            pltpu.VMEM((8, 16, W), BF),
            pltpu.VMEM((8, 2, W), F32),
            pltpu.SemaphoreType.DMA((144,)),
            pltpu.SemaphoreType.DMA((144,)),
        ],
        compiler_params=pltpu.CompilerParams(
            collective_id=0, has_side_effects=True, vmem_limit_bytes=56 * 1024 * 1024),
    )(source, target, enc_weight, enc_bias.reshape(1, 256), dec_weight.T, active)
    return (err, ge, gb.reshape(256), gd)


def solution(mesh):
    placed = (
        P(("tok", "feat"), None),
        P(("tok", "feat"), None),
        P("tok", "feat"),
        P("feat"),
        P("feat", "tok"),
        P("tok", "feat"),
    )
    return jax.shard_map(
        on_device,
        mesh=mesh,
        in_specs=placed,
        out_specs=(P(("tok", "feat"), None), P(None, "feat"), P("feat"), P("feat", None)),
        check_vma=False,
    )
```

time: 199 us -> 170 us (0.85)
  Pallas kernels: 190 us -> 163 us
    pallas_call x1, Pallas kernels: 190 us -> 163 us  [on_device(): pl.pallas_call(kernel, out_shape=(jax.ShapeDtypeStruct((2, 8 * W), F32),...]
    unnamed x7 -> x8, local copies, waits for them, and re-layouts: 4.78 us -> 6.14 us
where the time goes in v3:
time: 170 us
  Pallas kernels  163 us (96%)
  local copies, waits for them, and re-layouts  6.14 us (4%)
    pallas_call x1, Pallas kernels, on_device(): pl.pallas_call(kernel, out_shape=(jax.ShapeDtypeStruct((2, 8 * W), F32),...  163 us
    unnamed x8, local copies, waits for them, and re-layouts  6.14 us

profile of v3, /device:TPU:1, one launch (start us, length us, event | category | flops | bytes accessed | tf_op | source)
XLA Modules:
  0.0 169.7 jit_solution(7419887208102887792)
XLA Ops:
  0.6 163.0 %shard_map.93 = (f32[2,3584]{1,0:T(2,128)}, bf16[3584,256]{1,0:T(8,128)(2,1)}, f32[1,256]{1,0:T(1,128)}, bf16[256,3584]{1,0:T(8,128)(2,1)}) custom-call(bf16[2,3584]{1,0:T(2,128)(2,1)} %src_ref.1, bf16[2,3584]{1,0:T(2,128)(2,1)} %tgt_ref.1, bf16[448,256]{1,0:T(8,128)(2,1)} %enc_ref.1, f32[1,256]{1,0:T(1,128)} %bitcast.4, bf16[448,256]{1,0:T(8,128)(2,1)} %bitcast.3, ...), custom_call_target="tpu_custom_call" | custom-call | tf_op jit(solution)/shard_map/pallas_call | solution.py:310
  163.6 1.4 copy.14
  165.0 0.0 copy-start.1
  165.0 0.0 copy-start
  165.0 3.0 %copy.15 = bf16[3584,256]{1,0:T(8,128)(2,1)} copy(bf16[3584,256]{1,0:T(8,128)(2,1)} %get-tuple-element.17) | data formatting | bytes 3670016
  167.9 0.0 copy-done.1
  167.9 0.6 copy.16
  168.5 0.0 copy-done
  168.5 1.2 copy.17
Async XLA Ops:
  165.0 3.0 %copy-start.1 = (f32[1,256]{1,0:T(1,128)S(1)}, f32[1,256]{1,0:T(1,128)}, u32[]{:S(2)}) copy-start(f32[1,256]{1,0:T(1,128)} %get-tuple-element.10) | copy-start | bytes 3076
  165.0 3.6 %copy-start = (bf16[256,3584]{1,0:T(8,128)(2,1)S(1)}, bf16[256,3584]{1,0:T(8,128)(2,1)}, u32[]{:S(2)}) copy-start(bf16[256,3584]{1,0:T(8,128)(2,1)} %get-tuple-element.19) | copy-start | bytes 5505028

commit v4 on v3

--- a/solution.py
+++ b/solution.py
@@ -137,13 +137,13 @@
         st_rows[1, 2 * k:2 * k + 2, :] = v[2:4]
     S[zl, gi, zr] = st_rows[0].astype(BF)
     sz = far(S)
-    wz = [w_part(0)]
+    wz = [w_part(0), w_part(1)]
     arrive(sz)
     sn = near(S)
     w0l, w0f = ring_pass(w0)
     arrive(sn)
     one = light(S)
-    wz += [w_part(1), w_part(2), w_part(3)]
+    wz += [w_part(2), w_part(3)]
     arrive([az])
     apair = at.at[pl.ds(2 * x, 2)]
     ax = [send(apair, apair, dev(x_=(x + d) % 4)) for d in (1, 3, 2)]
@@ -155,9 +155,6 @@
     arrive(w0f)
     al, af = ring_pass(ra)
     bl, bf = ring_pass(rb)
-    arrive(wz)
-    w1 = ring_start(w_piece(wt, 1 - zh), "x_")
-    dz = send(dt.at[me], dt.at[me], across)
     arrive(ax)
 
     for h in range(2):
@@ -172,8 +169,9 @@
             acc += jnp.dot(perm, at[(t % 4) * 2 + t // 4], preferred_element_type=F32)
         gate[h] = acc
 
-    w1l, w1f = ring_pass(w1)
-    d0 = ring_start(w_piece(dt, zh), "x_")
+    dz = send(dt.at[me], dt.at[me], across)
+    arrive(wz)
+    w1 = ring_start(w_piece(wt, 1 - zh), "x_")
 
     def rows(buf, h, k):
         parts = []
@@ -182,15 +180,15 @@
             parts.append(buf[1, ((h * 4 + k // 2) * 4 + yy) * 2 + k % 2].reshape(64, W))
         return jnp.concatenate(parts, axis=0)
 
-    def encode(h):
-        pre[...] = jnp.zeros((512, 256), F32)
-
-        def step(k, _):
-            pre[...] += jnp.dot(rows(S, h, k), wt[k], preferred_element_type=F32)
+    def encode(h, side):
+        def step(i, _):
+            pre[h] += jnp.dot(rows(S, h, 2 * i + side), wt[2 * i + side], preferred_element_type=F32)
             return 0
 
-        lax.fori_loop(0, 8, step, 0)
-        feats[h] = (gate[h] * (pre[...] + bias_ref[...])).astype(BF)
+        lax.fori_loop(0, 4, step, 0)
+
+    def finish(h):
+        feats[h] = (gate[h] * (pre[h] + bias_ref[...])).astype(BF)
 
     def decode(h):
         r = lax.dot_general(feats[h], dt[me], (((1,), (1,)), ((), ())), preferred_element_type=F32)
@@ -203,17 +201,22 @@
     sc.append(swap(S, 0, (y + 2) % 4))
     arrive(bf)
     sc.append(swap(S, 1, (x + 2) % 4))
+    w1l, w1f = ring_pass(w1)
+    d0 = ring_start(w_piece(dt, zh), "x_")
+    pre[...] = jnp.zeros((2, 512, 256), F32)
+    encode(c, zh)
+    arrive(sc)
+    encode(1 - c, zh)
     arrive(w1l)
     arrive(w1f)
-    encode(c)
-    d0l, d0f = ring_pass(d0)
-    arrive(sc)
-    encode(1 - c)
+    encode(1 - c, 1 - zh)
+    finish(1 - c)
     decode(1 - c)
     pc = [send(part.at[1 - c, (y + d) % 4], r0.at[(y + d) % 4], dev(c_=1 - c)) for d in (2, 1, 3, 0)]
+    encode(c, 1 - zh)
+    finish(c)
+    d0l, d0f = ring_pass(d0)
     decode(c)
-    arrive([dz])
-    d1 = ring_start(w_piece(dt, 1 - zh), "x_")
     py = []
     for i, d in enumerate((2, 1, 3)):
         yy = (y + d) % 4
@@ -228,7 +231,8 @@
     part[c, y] = total
     qb[...] = total.astype(BF)
     pz = [send(qb.at[(zlo + d) % 8], r2.at[d], dev(z_=zh * 8 + (zlo + d) % 8)) for d in (4, 3, 5, 2, 6, 1, 7)]
-    d1l, d1f = ring_pass(d1)
+    arrive([dz])
+    d1 = ring_start(w_piece(dt, 1 - zh), "x_")
     arrive(pz)
     recon = part[c, y, zlo]
     for d in range(1, 8):
@@ -241,6 +245,7 @@
         ebuf[k] = err[2 * k:2 * k + 2]
     err_in[tok] = ebuf[tok]
     eo = [send(ebuf.at[(tok + d) % 8], err_in.at[tok], tok_dev(d)) for d in range(1, 8)]
+    d1l, d1f = ring_pass(d1)
     arrive(gz)
     arrive(near(G))
     arrive(light(G))
@@ -267,14 +272,14 @@
     gc.append(swap(G, 1, (x + 2) % 4))
 
     def back(h):
-        pre[...] = jnp.zeros((512, 256), F32)
+        pre[h] = jnp.zeros((512, 256), F32)
 
         def step(k, _):
-            pre[...] += jnp.dot(rows(G, h, k), dt[k], preferred_element_type=F32)
+            pre[h] += jnp.dot(rows(G, h, k), dt[k], preferred_element_type=F32)
             return 0
 
         lax.fori_loop(0, 8, step, 0)
-        g = gate[h] * pre[...]
+        g = gate[h] * pre[h]
         prnd[h] = g.astype(BF)
         return jnp.sum(g, axis=0, keepdims=True)
 
@@ -329,7 +334,7 @@
             pltpu.VMEM((8, W, 256), BF),
             pltpu.VMEM((8, W, 256), BF),
             pltpu.VMEM((2, 512, 256), F32),
-            pltpu.VMEM((512, 256), F32),
+            pltpu.VMEM((2, 512, 256), F32),
             pltpu.VMEM((2, 512, 256), BF),
             pltpu.VMEM((2, 256, 512), BF),
             pltpu.VMEM((2, 512, 256), BF),

time: 170 us -> 169 us (level)
  no operation moved by 1% of the time
where the time goes in v4:
time: 169 us
  Pallas kernels  162 us (96%)
  local copies, waits for them, and re-layouts  6.14 us (4%)
    pallas_call x1, Pallas kernels, on_device(): pl.pallas_call(kernel, out_shape=(jax.ShapeDtypeStruct((2, 8 * W), F32),...  162 us
    unnamed x8, local copies, waits for them, and re-layouts  6.14 us

profile of v4, /device:TPU:1, one launch (start us, length us, event | category | flops | bytes accessed | tf_op | source)
XLA Modules:
  0.0 168.6 jit_solution(12163114853353375935)
XLA Ops:
  0.6 161.8 %shard_map.93 = (f32[2,3584]{1,0:T(2,128)}, bf16[3584,256]{1,0:T(8,128)(2,1)}, f32[1,256]{1,0:T(1,128)}, bf16[256,3584]{1,0:T(8,128)(2,1)}) custom-call(bf16[2,3584]{1,0:T(2,128)(2,1)} %src_ref.1, bf16[2,3584]{1,0:T(2,128)(2,1)} %tgt_ref.1, bf16[448,256]{1,0:T(8,128)(2,1)} %enc_ref.1, f32[1,256]{1,0:T(1,128)} %bitcast.4, bf16[448,256]{1,0:T(8,128)(2,1)} %bitcast.3, ...), custom_call_target="tpu_custom_call" | custom-call | tf_op jit(solution)/shard_map/pallas_call | solution.py:315
  162.5 1.4 copy.14
  163.8 0.0 copy-start.1
  163.8 0.0 copy-start
  163.8 3.0 %copy.15 = bf16[3584,256]{1,0:T(8,128)(2,1)} copy(bf16[3584,256]{1,0:T(8,128)(2,1)} %get-tuple-element.17) | data formatting | bytes 3670016
  166.8 0.0 copy-done.1
  166.8 0.6 copy.16
  167.4 0.0 copy-done
  167.4 1.2 copy.17
Async XLA Ops:
  163.8 3.0 %copy-start.1 = (f32[1,256]{1,0:T(1,128)S(1)}, f32[1,256]{1,0:T(1,128)}, u32[]{:S(2)}) copy-start(f32[1,256]{1,0:T(1,128)} %get-tuple-element.10) | copy-start | bytes 3076
  163.8 3.6 %copy-start = (bf16[256,3584]{1,0:T(8,128)(2,1)S(1)}, bf16[256,3584]{1,0:T(8,128)(2,1)}, u32[]{:S(2)}) copy-start(bf16[256,3584]{1,0:T(8,128)(2,1)} %get-tuple-element.19) | copy-start | bytes 5505028

commit v5 on v4

--- a/solution.py
+++ b/solution.py
@@ -140,35 +140,36 @@
     wz = [w_part(0), w_part(1)]
     arrive(sz)
     sn = near(S)
+    arrive([az])
+    apair = at.at[pl.ds(2 * x, 2)]
+    ax = [send(apair, apair, dev(x_=(x + d) % 4)) for d in (1, 3, 2)]
     w0l, w0f = ring_pass(w0)
     arrive(sn)
     one = light(S)
     wz += [w_part(2), w_part(3)]
-    arrive([az])
-    apair = at.at[pl.ds(2 * x, 2)]
-    ax = [send(apair, apair, dev(x_=(x + d) % 4)) for d in (1, 3, 2)]
     arrive(one)
     ra = ring_start(heavy(S, 0), "y_")
     rb = ring_start(heavy(S, 1), "x_")
     sc = [swap(S, 0, y), swap(S, 1, x)]
+    arrive(ax)
+
+    def order(h):
+        n = lax.broadcasted_iota(jnp.int32, (512, 128), 0)
+        m = lax.broadcasted_iota(jnp.int32, (512, 128), 1)
+        fidx = ((((n >> 4) & 7) * 4 + (n >> 7)) * 2) + h
+        slot = jnp.where(m == fidx * 2 + (n & 1), (n >> 1) & 7, 8)
+        acc = jnp.zeros((512, 256), F32)
+        for t in range(8):
+            perm = jnp.where(slot == t, 1.0, 0.0).astype(BF)
+            acc += jnp.dot(perm, at[(t % 4) * 2 + t // 4], preferred_element_type=F32)
+        gate[h] = acc
+
+    order(0)
+    al, af = ring_pass(ra)
+    bl, bf = ring_pass(rb)
+    order(1)
     arrive(w0l)
     arrive(w0f)
-    al, af = ring_pass(ra)
-    bl, bf = ring_pass(rb)
-    arrive(ax)
-
-    for h in range(2):
-        n = lax.broadcasted_iota(jnp.int32, (512, 128), 0)
-        m = lax.broadcasted_iota(jnp.int32, (512, 128), 1)
-        fidx = (((n // 16) % 8) * 4 + n // 128) * 2 + h
-        want = fidx * 2 + n % 2
-        tn = (n // 2) % 8
-        acc = jnp.zeros((512, 256), F32)
-        for t in range(8):
-            perm = jnp.where((m == want) & (tn == t), 1.0, 0.0).astype(BF)
-            acc += jnp.dot(perm, at[(t % 4) * 2 + t // 4], preferred_element_type=F32)
-        gate[h] = acc
-
     dz = send(dt.at[me], dt.at[me], across)
     arrive(wz)
     w1 = ring_start(w_piece(wt, 1 - zh), "x_")
@@ -224,8 +225,13 @@
         pb[yy] = (part[c, yy] + r0[yy]).astype(BF)
         py.append(send(pb.at[yy], r1.at[d], dev(y_=yy)))
     arrive([pc[3]])
+    def turn(k, _):
+        ST[k] = jnp.concatenate([rows(S, 0, k), rows(S, 1, k)], axis=0).T
+        return 0
+
     for h in range(2):
         fT[h] = feats[h].T
+    lax.fori_loop(0, 1, turn, 0)
     arrive(py)
     total = part[c, y] + r0[y] + r1[1].astype(F32) + r1[2].astype(F32) + r1[3].astype(F32)
     part[c, y] = total
@@ -233,6 +239,7 @@
     pz = [send(qb.at[(zlo + d) % 8], r2.at[d], dev(z_=zh * 8 + (zlo + d) % 8)) for d in (4, 3, 5, 2, 6, 1, 7)]
     arrive([dz])
     d1 = ring_start(w_piece(dt, 1 - zh), "x_")
+    lax.fori_loop(1, 4, turn, 0)
     arrive(pz)
     recon = part[c, y, zlo]
     for d in range(1, 8):
@@ -246,6 +253,7 @@
     err_in[tok] = ebuf[tok]
     eo = [send(ebuf.at[(tok + d) % 8], err_in.at[tok], tok_dev(d)) for d in range(1, 8)]
     d1l, d1f = ring_pass(d1)
+    lax.fori_loop(4, 6, turn, 0)
     arrive(gz)
     arrive(near(G))
     arrive(light(G))
@@ -253,11 +261,7 @@
     rb = ring_start(heavy(G, 1), "x_")
     gc = [swap(G, 0, y), swap(G, 1, x)]
 
-    def turn(k, _):
-        ST[k] = jnp.concatenate([rows(S, 0, k), rows(S, 1, k)], axis=0).T
-        return 0
-
-    lax.fori_loop(0, 4, turn, 0)
+    lax.fori_loop(6, 8, turn, 0)
     al, af = ring_pass(ra)
     bl, bf = ring_pass(rb)
     for cps in (d0l, d0f, d1l, d1f):
@@ -265,7 +269,6 @@
     arrive(al)
     arrive(bl)
     gc += [swap(G, 0, (y + 1) % 4), swap(G, 0, (y + 3) % 4), swap(G, 1, (x + 1) % 4), swap(G, 1, (x + 3) % 4)]
-    lax.fori_loop(4, 8, turn, 0)
     arrive(af)
     gc.append(swap(G, 0, (y + 2) % 4))
     arrive(bf)

time: 169 us -> 167 us (0.988)
  Pallas kernels: 162 us -> 160 us
    pallas_call x1, Pallas kernels: 162 us -> 160 us  [on_device(): pl.pallas_call(kernel, out_shape=(jax.ShapeDtypeStruct((2, 8 * W), F32),...]
where the time goes in v5:
time: 167 us
  Pallas kernels  160 us (96%)
  local copies, waits for them, and re-layouts  6.14 us (4%)
    pallas_call x1, Pallas kernels, on_device(): pl.pallas_call(kernel, out_shape=(jax.ShapeDtypeStruct((2, 8 * W), F32),...  160 us
    unnamed x8, local copies, waits for them, and re-layouts  6.14 us

profile of v5, /device:TPU:1, one launch (start us, length us, event | category | flops | bytes accessed | tf_op | source)
XLA Modules:
  0.0 166.6 jit_solution(689083682258587863)
XLA Ops:
  0.6 159.9 %shard_map.93 = (f32[2,3584]{1,0:T(2,128)}, bf16[3584,256]{1,0:T(8,128)(2,1)}, f32[1,256]{1,0:T(1,128)}, bf16[256,3584]{1,0:T(8,128)(2,1)}) custom-call(bf16[2,3584]{1,0:T(2,128)(2,1)} %src_ref.1, bf16[2,3584]{1,0:T(2,128)(2,1)} %tgt_ref.1, bf16[448,256]{1,0:T(8,128)(2,1)} %enc_ref.1, f32[1,256]{1,0:T(1,128)} %bitcast.4, bf16[448,256]{1,0:T(8,128)(2,1)} %bitcast.3, ...), custom_call_target="tpu_custom_call" | custom-call | tf_op jit(solution)/shard_map/pallas_call | solution.py:318
  160.5 1.4 copy.14
  161.9 0.0 copy-start.1
  161.9 0.0 copy-start
  161.9 3.0 %copy.15 = bf16[3584,256]{1,0:T(8,128)(2,1)} copy(bf16[3584,256]{1,0:T(8,128)(2,1)} %get-tuple-element.17) | data formatting | bytes 3670016
  164.8 0.0 copy-done.1
  164.8 0.6 copy.16
  165.4 0.0 copy-done
  165.4 1.2 copy.17
Async XLA Ops:
  161.9 3.0 %copy-start.1 = (f32[1,256]{1,0:T(1,128)S(1)}, f32[1,256]{1,0:T(1,128)}, u32[]{:S(2)}) copy-start(f32[1,256]{1,0:T(1,128)} %get-tuple-element.10) | copy-start | bytes 3076
  161.9 3.6 %copy-start = (bf16[256,3584]{1,0:T(8,128)(2,1)S(1)}, bf16[256,3584]{1,0:T(8,128)(2,1)}, u32[]{:S(2)}) copy-start(bf16[256,3584]{1,0:T(8,128)(2,1)} %get-tuple-element.19) | copy-start | bytes 5505028

commit v6 on v5

--- a/solution.py
+++ b/solution.py
@@ -186,7 +186,7 @@
             pre[h] += jnp.dot(rows(S, h, 2 * i + side), wt[2 * i + side], preferred_element_type=F32)
             return 0
 
-        lax.fori_loop(0, 4, step, 0)
+        lax.fori_loop(0, 4, step, 0, unroll=2)
 
     def finish(h):
         feats[h] = (gate[h] * (pre[h] + bias_ref[...])).astype(BF)
@@ -230,7 +230,7 @@
         return 0
 
     for h in range(2):
-        fT[h] = feats[h].T
+        fT[:, h * 512:h * 512 + 512] = feats[h].T
     lax.fori_loop(0, 1, turn, 0)
     arrive(py)
     total = part[c, y] + r0[y] + r1[1].astype(F32) + r1[2].astype(F32) + r1[3].astype(F32)
@@ -281,7 +281,7 @@
             pre[h] += jnp.dot(rows(G, h, k), dt[k], preferred_element_type=F32)
             return 0
 
-        lax.fori_loop(0, 8, step, 0)
+        lax.fori_loop(0, 8, step, 0, unroll=2)
         g = gate[h] * pre[h]
         prnd[h] = g.astype(BF)
         return jnp.sum(g, axis=0, keepdims=True)
@@ -295,11 +295,9 @@
         for odd in range(2):
             t = 2 * n + odd
             k = (t % 4) * 2 + t // 4
-            ge = jnp.zeros((W, 256), F32)
-            gd = jnp.zeros((256, W), F32)
-            for h in range(2):
-                ge += jnp.dot(ST[k, :, h * 512:h * 512 + 512], prnd[h], preferred_element_type=F32)
-                gd += jnp.dot(fT[h], rows(G, h, k), preferred_element_type=F32)
+            ge = jnp.dot(ST[k], prnd[...].reshape(1024, 256), preferred_element_type=F32)
+            gd = jnp.dot(fT[...], jnp.concatenate([rows(G, 0, k), rows(G, 1, k)], axis=0),
+                         preferred_element_type=F32)
             ge_ref[pl.ds(pl.multiple_of(t * W, W), W), :] = ge.astype(BF)
             halves.append(gd)
         both = jnp.concatenate(halves, axis=1).astype(BF)
@@ -339,7 +337,7 @@
             pltpu.VMEM((2, 512, 256), F32),
             pltpu.VMEM((2, 512, 256), F32),
             pltpu.VMEM((2, 512, 256), BF),
-            pltpu.VMEM((2, 256, 512), BF),
+            pltpu.VMEM((256, 1024), BF),
             pltpu.VMEM((2, 512, 256), BF),
             pltpu.VMEM((2, 4, 8, 16, W), F32),
             pltpu.VMEM((4, 8, 16, W), F32),

time: 167 us -> 166 us (level)
  no operation moved by 1% of the time
where the time goes in v6:
time: 166 us
  Pallas kernels  159 us (96%)
  local copies, waits for them, and re-layouts  6.14 us (4%)
    pallas_call x1, Pallas kernels, on_device(): pl.pallas_call(kernel, out_shape=(jax.ShapeDtypeStruct((2, 8 * W), F32),...  159 us
    unnamed x8, local copies, waits for them, and re-layouts  6.14 us

profile of v6, /device:TPU:1, one launch (start us, length us, event | category | flops | bytes accessed | tf_op | source)
XLA Modules:
  0.0 165.7 jit_solution(10383109062964144325)
XLA Ops:
  0.6 158.9 %shard_map.93 = (f32[2,3584]{1,0:T(2,128)}, bf16[3584,256]{1,0:T(8,128)(2,1)}, f32[1,256]{1,0:T(1,128)}, bf16[256,3584]{1,0:T(8,128)(2,1)}) custom-call(bf16[2,3584]{1,0:T(2,128)(2,1)} %src_ref.1, bf16[2,3584]{1,0:T(2,128)(2,1)} %tgt_ref.1, bf16[448,256]{1,0:T(8,128)(2,1)} %enc_ref.1, f32[1,256]{1,0:T(1,128)} %bitcast.4, bf16[448,256]{1,0:T(8,128)(2,1)} %bitcast.3, ...), custom_call_target="tpu_custom_call" | custom-call | tf_op jit(solution)/shard_map/pallas_call | solution.py:316
  159.6 1.4 copy.14
  160.9 0.0 copy-start.1
  160.9 0.0 copy-start
  160.9 3.0 %copy.15 = bf16[3584,256]{1,0:T(8,128)(2,1)} copy(bf16[3584,256]{1,0:T(8,128)(2,1)} %get-tuple-element.17) | data formatting | bytes 3670016
  163.9 0.0 copy-done.1
  163.9 0.6 copy.16
  164.5 0.0 copy-done
  164.5 1.2 copy.17
Async XLA Ops:
  160.9 3.0 %copy-start.1 = (f32[1,256]{1,0:T(1,128)S(1)}, f32[1,256]{1,0:T(1,128)}, u32[]{:S(2)}) copy-start(f32[1,256]{1,0:T(1,128)} %get-tuple-element.10) | copy-start | bytes 3076
  160.9 3.6 %copy-start = (bf16[256,3584]{1,0:T(8,128)(2,1)S(1)}, bf16[256,3584]{1,0:T(8,128)(2,1)}, u32[]{:S(2)}) copy-start(bf16[256,3584]{1,0:T(8,128)(2,1)} %get-tuple-element.19) | copy-start | bytes 5505028

commit v7 on v6

--- a/solution.py
+++ b/solution.py
@@ -167,12 +167,12 @@
     order(0)
     al, af = ring_pass(ra)
     bl, bf = ring_pass(rb)
-    order(1)
     arrive(w0l)
     arrive(w0f)
     dz = send(dt.at[me], dt.at[me], across)
     arrive(wz)
     w1 = ring_start(w_piece(wt, 1 - zh), "x_")
+    order(1)
 
     def rows(buf, h, k):
         parts = []

time: 166 us -> 166 us (level)
  no operation moved by 1% of the time
where the time goes in v7:
time: 166 us
  Pallas kernels  159 us (96%)
  local copies, waits for them, and re-layouts  6.14 us (4%)
    pallas_call x1, Pallas kernels, on_device(): pl.pallas_call(kernel, out_shape=(jax.ShapeDtypeStruct((2, 8 * W), F32),...  159 us
    unnamed x8, local copies, waits for them, and re-layouts  6.14 us

profile of v7, /device:TPU:1, one launch (start us, length us, event | category | flops | bytes accessed | tf_op | source)
XLA Modules:
  0.0 165.7 jit_solution(15818784644025068333)
XLA Ops:
  0.6 158.9 %shard_map.93 = (f32[2,3584]{1,0:T(2,128)}, bf16[3584,256]{1,0:T(8,128)(2,1)}, f32[1,256]{1,0:T(1,128)}, bf16[256,3584]{1,0:T(8,128)(2,1)}) custom-call(bf16[2,3584]{1,0:T(2,128)(2,1)} %src_ref.1, bf16[2,3584]{1,0:T(2,128)(2,1)} %tgt_ref.1, bf16[448,256]{1,0:T(8,128)(2,1)} %enc_ref.1, f32[1,256]{1,0:T(1,128)} %bitcast.4, bf16[448,256]{1,0:T(8,128)(2,1)} %bitcast.3, ...), custom_call_target="tpu_custom_call" | custom-call | tf_op jit(solution)/shard_map/pallas_call | solution.py:316
  159.6 1.4 copy.14
  160.9 0.0 copy-start.1
  160.9 0.0 copy-start
  160.9 3.0 %copy.15 = bf16[3584,256]{1,0:T(8,128)(2,1)} copy(bf16[3584,256]{1,0:T(8,128)(2,1)} %get-tuple-element.17) | data formatting | bytes 3670016
  163.9 0.0 copy-done.1
  163.9 0.6 copy.16
  164.5 0.0 copy-done
  164.5 1.2 copy.17
Async XLA Ops:
  160.9 3.0 %copy-start.1 = (f32[1,256]{1,0:T(1,128)S(1)}, f32[1,256]{1,0:T(1,128)}, u32[]{:S(2)}) copy-start(f32[1,256]{1,0:T(1,128)} %get-tuple-element.10) | copy-start | bytes 3076
  160.9 3.6 %copy-start = (bf16[256,3584]{1,0:T(8,128)(2,1)S(1)}, bf16[256,3584]{1,0:T(8,128)(2,1)}, u32[]{:S(2)}) copy-start(bf16[256,3584]{1,0:T(8,128)(2,1)} %get-tuple-element.19) | copy-start | bytes 5505028
